TPU v7x, 32 devices: a whole 2x2x4 slice. The times are simulated.
32 devices in a mesh: space: 16 (over z, y, core), mode: 2 (over x).
Axes of the slice: x: 2, y: 2, z: 4, core: 2. Of those that a mesh axis runs over, the one named last changes fastest.
Arguments:
- guess: float32 [120, 32, 8, 128], P('mode', 'space'), may hold values from -6 to 6
- source: float32 [120, 32, 8, 128], P('mode', 'space'), may hold values from -6 to 6
- mean_coef: float32 [32, 8, 128], P('space'), may hold values from 1 to 4
- fluct_coef: float32 [7, 32, 8, 128], P(None, 'space'), may hold values from -2 to 2
- triples: int32 [3, 1680], replicated, may hold values from 0 to 119, as said below
- coupling: float32 [1680], replicated, may hold values from -1.5 to 1.5
Outputs:
- solution: float32 [120, 32, 8, 128], P('mode', 'space')
- update: float32 [120, 32, 8, 128], P('mode', 'space')
Inputs may be any that keep to these rules, and one draw needn't show every extreme that they name: `triples`: row 0 holds the output mode i, row 1 the coupled mode j, row 2 the term k, which is 1 to 7; every pair (i, k) stands in exactly 2 entries, in no particular order; j is any mode.
All inputs are finite; a program needn't handle non-finite values.
Results may differ from a plain program's by a relative error of at most 0.00019.
Values sent between devices are 32-bit elements; how exact they have to be, the bound alone decides.
A program may use at most 64 MiB of HBM per device.

v0:
```python
import functools

import jax
import jax.numpy as jnp
from jax import lax
from jax.experimental import pallas as pl
from jax.experimental.pallas import tpu as pltpu
from jax.sharding import PartitionSpec as P

ITERS = 3
MESH = pl.DeviceIdType.MESH
SUB = 8
ROWS = 32


def kernel(dims, guess, source, mean, fluct, triples, coupling, sol_out, upd_out,
           field, rhs, pack_g, pack_s, back_s, back_u, last, coef, tile, faces, inverse,
           pattern, table, fine, coarse, plain,
           coef_sem, guess_sem, rhs_sem, rim_sem, x_sem, y_sem, sol_sem, upd_sem):
    slabs, groups, blocks, room, planes, rows, depth, terms, entries = dims
    share = rows // groups
    width = room * groups
    f32, bf16 = jnp.float32, jnp.bfloat16
    here = lax.axis_index("space")
    me = lax.axis_index("mode")
    has_prev, has_next = here > 0, here < slabs - 1
    has_left, has_right = me > 0, me < groups - 1
    even = lax.rem(here, 2) == 0

    def remote(src, dst, sems, index, space, mode):
        return pltpu.make_async_remote_copy(
            src_ref=src, dst_ref=dst, send_sem=sems.at[(0,) + index], recv_sem=sems.at[(1,) + index],
            device_id={"space": space, "mode": mode}, device_id_type=MESH)

    def group(offset):
        return lax.rem(me + offset + groups, groups)

    def block(owner):
        return pl.ds(pl.multiple_of(owner * room, SUB), room)

    def plane_at(q):
        return jnp.where(even, planes - 1 - q, q)

    @pl.when(here == 0)
    def _():
        field[:, 0] = jnp.zeros((ITERS, share + 2, width, depth), f32)
        coef[:, 0] = jnp.zeros((terms, rows, depth), f32)

    @pl.when(here == slabs - 1)
    def _():
        field[:, planes + 1] = jnp.zeros((ITERS, share + 2, width, depth), f32)
        coef[:, planes + 1] = jnp.zeros((terms, rows, depth), f32)

    @pl.when(me == 0)
    def _():
        field[:, 1:planes + 1, 0] = jnp.zeros((ITERS, planes, width, depth), f32)

    @pl.when(me == groups - 1)
    def _():
        field[:, 1:planes + 1, share + 1] = jnp.zeros((ITERS, planes, width, depth), f32)

    barrier = pltpu.get_barrier_semaphore()

    @pl.when(has_prev)
    def _():
        pl.semaphore_signal(barrier, inc=1, device_id={"space": here - 1, "mode": me}, device_id_type=MESH)

    @pl.when(has_next)
    def _():
        pl.semaphore_signal(barrier, inc=1, device_id={"space": here + 1, "mode": me}, device_id_type=MESH)

    for d in range(1, groups):
        pl.semaphore_signal(barrier, inc=1, device_id={"space": here, "mode": group(d)}, device_id_type=MESH)

    tall = share + 1 if groups == 2 else share + 2

    def first_row(owner):
        return jnp.where(owner > 0, 0, 1) if groups == 2 else 0

    gap = jnp.zeros((room - blocks, depth), f32)

    def rows_of(ref, p, y):
        part = ref[pl.ds(p * rows + y, blocks, stride=planes * rows), :]
        return jnp.concatenate([part, gap], axis=0) if room > blocks else part

    for t in range(groups):
        for p in range(planes):
            for r in range(share + 2):
                y = t * share + r - 1
                if 0 <= y < rows:
                    pack_g[t, p, r] = rows_of(guess, p, y)
                elif groups != 2:
                    pack_g[t, p, r] = jnp.zeros((room, depth), f32)

    pl.semaphore_wait(barrier, groups - 1 + has_prev.astype(jnp.int32) + has_next.astype(jnp.int32))

    def coef_copies(up):
        at, to, space = (planes - 1, 0, here + 1) if up else (0, planes + 1, here - 1)
        way = 0 if up else 1
        return [
            remote(mean.at[at], coef.at[0, to], coef_sem, (way, 0), space, me),
            remote(fluct.at[:, at], coef.at[pl.ds(1, terms - 1), to], coef_sem, (way, 1), space, me),
        ]

    def guess_copy(d, p, owner, target):
        start = first_row(target)
        return remote(
            pack_g.at[target, p, pl.ds(start, tall)],
            field.at[0, p + 1, pl.ds(start, tall), block(owner)],
            guess_sem, (d, p), here, target)

    for q in range(planes):
        p = plane_at(planes - 1 - q)
        for d in range(1, groups):
            guess_copy(d, p, me, group(d)).start()

    @pl.when(has_next)
    def _():
        for copy in coef_copies(True):
            copy.start()

    @pl.when(has_prev)
    def _():
        for copy in coef_copies(False):
            copy.start()

    def rim_copy(up, d, owner):
        at, to, space = (planes, 0, here + 1) if up else (1, planes + 1, here - 1)
        span = pl.ds(1, share)
        return remote(field.at[0, at, span, block(owner)], field.at[0, to, span, block(owner)],
                      rim_sem, (0 if up else 1, d), space, me)

    for p in range(planes):
        for r in range(tall):
            at = first_row(me) + r
            field[0, p + 1, at, block(me)] = pack_g[me, p, at]

    @pl.when(has_next)
    def _():
        rim_copy(True, 0, me).start()

    @pl.when(has_prev)
    def _():
        rim_copy(False, 0, me).start()

    for t in range(groups):
        for p in range(planes):
            for r in range(share):
                pack_s[t, p, r] = rows_of(source, p, t * share + r)
    rhs[:, :, block(me)] = pack_s[me]

    pattern[...] = jnp.full(pattern.shape, -1, jnp.int32)
    pattern[0:3, 0:entries] = triples[...]
    length = pattern.shape[1]

    def spread(i):
        shift = jnp.zeros_like(i)
        for g in range(1, groups):
            shift = shift + jnp.where(i >= g * blocks, room - blocks, 0)
        return i + shift

    owner_row = spread(pattern[0:1, :])
    column = spread(pattern[1:2, :]) + (pattern[2:3, :] - 1) * width
    value = jnp.concatenate([coupling[...], jnp.zeros((1, length - entries), f32)], axis=1)
    high = value.astype(bf16).astype(f32)
    low = value - high
    hit = lax.broadcasted_iota(jnp.int32, (width, length), 0) == owner_row
    picks = jnp.concatenate(
        [jnp.where(hit, high, 0.0).astype(bf16), jnp.where(hit, low, 0.0).astype(bf16)], axis=0)

    for k in range(terms - 1):
        chosen = lax.broadcasted_iota(jnp.int32, (width, length), 0) + k * width == column
        chosen = jnp.where(chosen, 1.0, 0.0).astype(bf16)
        both = lax.dot_general(picks, chosen, (((1,), (1,)), ((), ())), preferred_element_type=f32)
        entry = both[:width] + both[width:]
        top = entry.astype(bf16)
        table[:width, k * width:(k + 1) * width] = top
        table[width:, k * width:(k + 1) * width] = (entry - top.astype(f32)).astype(bf16)

    def rhs_copy(d, owner, target):
        return remote(pack_s.at[target], rhs.at[:, :, block(owner)], rhs_sem, (d,), here, target)

    for d in range(1, groups):
        owner = group(-d)
        for p in range(planes):
            guess_copy(d, p, owner, me).wait_recv()

        @pl.when(has_next)
        def _():
            rim_copy(True, d, owner).start()

        @pl.when(has_prev)
        def _():
            rim_copy(False, d, owner).start()

    for d in range(1, groups):
        rhs_copy(d, me, group(d)).start()

    coef[0, 1:planes + 1] = mean[...]
    coef[1:, 1:planes + 1] = fluct[...]

    @pl.when(has_prev)
    def _():
        for copy in coef_copies(True):
            copy.wait_recv()

    @pl.when(has_next)
    def _():
        for copy in coef_copies(False):
            copy.wait_recv()

    def face_step(k, p):
        a = coef[k, p + 1]
        row = lax.broadcasted_iota(jnp.int32, a.shape, 0)
        lane = lax.broadcasted_iota(jnp.int32, a.shape, 1)
        tile[0] = 0.5 * (a + coef[k, p + 2])
        tile[1] = 0.5 * (a + coef[k, p])
        tile[2] = 0.5 * (a + jnp.where(row == rows - 1, 0.0, pltpu.roll(a, rows - 1, 0)))
        tile[3] = 0.5 * (a + jnp.where(row == 0, 0.0, pltpu.roll(a, 1, 0)))
        tile[4] = 0.5 * (a + jnp.where(lane == depth - 1, 0.0, pltpu.roll(a, depth - 1, 1)))
        tile[5] = 0.5 * (a + jnp.where(lane == 0, 0.0, pltpu.roll(a, 1, 1)))
        for r in range(share):
            for n in range(6):
                faces[p, r, k, n] = jnp.broadcast_to(tile[n, pl.ds(me * share + r, 1), :], (SUB, depth))

    def face_loop(k, carry):
        for p in range(planes):
            face_step(k, p)
        return carry

    lax.fori_loop(0, terms, face_loop, 0)
    for p in range(planes):
        for r in range(share):
            total = faces[p, r, 0, 0]
            for n in range(1, 6):
                total = total + faces[p, r, 0, n]
            inverse[p, r] = 1.0 / total

    lane = lax.broadcasted_iota(jnp.int32, (ROWS, depth), 1)

    def gather_terms(step, p):
        def by_block(index, carry):
            r = index // (width // ROWS)
            begin = pl.multiple_of(lax.rem(index, width // ROWS) * ROWS, ROWS)

            def cells(a, b):
                return field[step, a, b, pl.ds(begin, ROWS), :]

            centre = cells(p + 1, r + 1)
            others = [
                cells(p + 2, r + 1), cells(p, r + 1), cells(p + 1, r + 2), cells(p + 1, r),
                jnp.where(lane == depth - 1, 0.0, pltpu.roll(centre, depth - 1, 1)),
                jnp.where(lane == 0, 0.0, pltpu.roll(centre, 1, 1)),
            ]
            drops = [(centre - other).reshape(ROWS // SUB, SUB, depth) for other in others]
            for k in range(terms):
                acc = faces[p, r, k, 0][None] * drops[0]
                for n in range(1, 6):
                    acc = acc + faces[p, r, k, n][None] * drops[n]
                acc = acc.reshape(ROWS, depth)
                if k == 0:
                    plain[r, pl.ds(begin, ROWS), :] = acc
                else:
                    top = acc.astype(bf16)
                    at = pl.ds(pl.multiple_of((k - 1) * width + begin, ROWS), ROWS)
                    lanes = pl.ds(pl.multiple_of(r * depth, depth), depth)
                    coarse[at, lanes] = top
                    fine[at, lanes] = (acc - top.astype(f32)).astype(bf16)
            return carry

        lax.fori_loop(0, share * (width // ROWS), by_block, 0)

    def x_copy(step, up):
        at, to, space = (planes, 0, here + 1) if up else (1, planes + 1, here - 1)
        span = pl.ds(1, share)
        return remote(field.at[step, at, span], field.at[step, to, span],
                      x_sem, (step, 0 if up else 1), space, me)

    def y_copy(step, p, right):
        at, to, mode = (share, 0, me + 1) if right else (1, share + 1, me - 1)
        return remote(field.at[step, p + 1, at], field.at[step, p + 1, to],
                      y_sem, (step, 0 if right else 1, p), here, mode)

    def sol_copy(d, p, slot, target):
        return remote(field.at[ITERS - 1, p + 1, pl.ds(1, share), block(target)], back_s.at[slot, p],
                      sol_sem, (d, p), here, target)

    def upd_copy(d, p, slot, target):
        return remote(last.at[p, :, block(target)], back_u.at[slot, p], upd_sem, (d, p), here, target)

    def await_rims(step, p):
        @pl.when((p == 0) & has_prev)
        def _():
            if step == 0:
                for d in range(groups):
                    rim_copy(True, d, group(-d)).wait_recv()
            else:
                x_copy(step, True).wait_recv()

        @pl.when((p == planes - 1) & has_next)
        def _():
            if step == 0:
                for d in range(groups):
                    rim_copy(False, d, group(-d)).wait_recv()
            else:
                x_copy(step, False).wait_recv()

        if step > 0:
            @pl.when(has_left)
            def _():
                y_copy(step, p, True).wait_recv()

            @pl.when(has_right)
            def _():
                y_copy(step, p, False).wait_recv()

    for step in range(ITERS):
        def sweep(q, carry, step=step):
            p = plane_at(q)
            await_rims(step, p)
            gather_terms(step, p)
            both = jnp.dot(table[...], coarse[...], preferred_element_type=f32)
            image = both[:width] + both[width:]
            image = image + jnp.dot(table[:width], fine[...], preferred_element_type=f32)
            if step == 0:
                @pl.when(q == 0)
                def _():
                    for d in range(1, groups):
                        rhs_copy(d, group(-d), me).wait_recv()
            for r in range(share):
                rest = rhs[p, r] - plain[r] - image[:, r * depth:(r + 1) * depth]
                rest = rest.reshape(width // SUB, SUB, depth) * inverse[p, r][None]
                rest = rest.reshape(width, depth)
                if step < ITERS - 1:
                    field[step + 1, p + 1, r + 1] = field[step, p + 1, r + 1] + 0.5 * rest
                else:
                    last[p, r] = rest
            if step < ITERS - 1:
                @pl.when((p == planes - 1) & has_next)
                def _():
                    x_copy(step + 1, True).start()

                @pl.when((p == 0) & has_prev)
                def _():
                    x_copy(step + 1, False).start()

                @pl.when(has_right)
                def _():
                    y_copy(step + 1, p, True).start()

                @pl.when(has_left)
                def _():
                    y_copy(step + 1, p, False).start()

            if step == ITERS - 2:
                for d in range(1, groups):
                    sol_copy(d, p, me, group(d)).start()
            if step == ITERS - 1:
                for d in range(1, groups):
                    upd_copy(d, p, me, group(d)).start()
            return carry

        lax.fori_loop(0, planes, sweep, 0)

    for p in range(planes):
        back_s[me, p] = field[ITERS - 1, p + 1, 1:share + 1, block(me)]
        back_u[me, p] = last[p, :, block(me)]
    for d in range(1, groups):
        for p in range(planes):
            sol_copy(d, p, group(-d), me).wait_recv()
            upd_copy(d, p, group(-d), me).wait_recv()
    for g in range(groups):
        for p in range(planes):
            for r in range(share):
                at = pl.ds(p * rows + g * share + r, blocks, stride=planes * rows)
                change = back_u[g, p, r][:blocks]
                upd_out[at, :] = change
                sol_out[at, :] = back_s[g, p, r][:blocks] + 0.5 * change

    for d in range(1, groups):
        for p in range(planes):
            guess_copy(d, p, me, group(d)).wait_send()
            sol_copy(d, p, me, group(d)).wait_send()
            upd_copy(d, p, me, group(d)).wait_send()
        rhs_copy(d, me, group(d)).wait_send()
    for up, has in ((True, has_next), (False, has_prev)):
        @pl.when(has)
        def _():
            for copy in coef_copies(up):
                copy.wait_send()
            for d in range(groups):
                rim_copy(up, d, group(-d)).wait_send()
            for step in range(1, ITERS):
                x_copy(step, up).wait_send()
    for right, has in ((True, has_right), (False, has_left)):
        @pl.when(has)
        def _():
            for step in range(1, ITERS):
                for p in range(planes):
                    y_copy(step, p, right).wait_send()


def per_device(guess, source, mean_coef, fluct_coef, triples, coupling):
    blocks, planes, rows, depth = guess.shape
    groups, slabs = lax.axis_size("mode"), lax.axis_size("space")
    terms = fluct_coef.shape[0] + 1
    entries = triples.shape[1]
    share = rows // groups
    room = -(-blocks // 16) * 16
    while (room * groups) % 128:
        room += 16
    width = room * groups
    length = -(-entries // 128) * 128
    f32, bf16 = jnp.float32, jnp.bfloat16
    dims = (slabs, groups, blocks, room, planes, rows, depth, terms, entries)
    flat = jax.ShapeDtypeStruct((blocks * planes * rows, depth), f32)
    dma = pltpu.SemaphoreType.DMA
    vmem = pl.BlockSpec(memory_space=pltpu.VMEM)
    solution, update = pl.pallas_call(
        functools.partial(kernel, dims),
        out_shape=(flat, flat),
        in_specs=[vmem] * 6,
        out_specs=(vmem, vmem),
        scratch_shapes=[
            pltpu.VMEM((ITERS, planes + 2, share + 2, width, depth), f32),
            pltpu.VMEM((planes, share, width, depth), f32),
            pltpu.VMEM((groups, planes, share + 2, room, depth), f32),
            pltpu.VMEM((groups, planes, share, room, depth), f32),
            pltpu.VMEM((groups, planes, share, room, depth), f32),
            pltpu.VMEM((groups, planes, share, room, depth), f32),
            pltpu.VMEM((planes, share, width, depth), f32),
            pltpu.VMEM((terms, planes + 2, rows, depth), f32),
            pltpu.VMEM((6, rows, depth), f32),
            pltpu.VMEM((planes, share, terms, 6, SUB, depth), f32),
            pltpu.VMEM((planes, share, SUB, depth), f32),
            pltpu.VMEM((SUB, length), jnp.int32),
            pltpu.VMEM((2 * width, (terms - 1) * width), bf16),
            pltpu.VMEM(((terms - 1) * width, share * depth), bf16),
            pltpu.VMEM(((terms - 1) * width, share * depth), bf16),
            pltpu.VMEM((share, width, depth), f32),
            dma((2, 2, 2)),
            dma((2, groups, planes)),
            dma((2, groups)),
            dma((2, 2, groups)),
            dma((2, ITERS, 2)),
            dma((2, ITERS, 2, planes)),
            dma((2, groups, planes)),
            dma((2, groups, planes)),
        ],
        compiler_params=pltpu.CompilerParams(
            collective_id=0, has_side_effects=True, vmem_limit_bytes=48 * 1024 * 1024
        ),
    )(
        guess.reshape(flat.shape),
        source.reshape(flat.shape),
        mean_coef,
        fluct_coef,
        triples,
        coupling.reshape(1, entries),
    )
    return solution.reshape(guess.shape), update.reshape(guess.shape)


def solution(mesh):
    in_specs = (
        P("mode", "space", None, None),
        P("mode", "space", None, None),
        P("space", None, None),
        P(None, "space", None, None),
        P(),
        P(),
    )
    out_specs = (P("mode", "space", None, None), P("mode", "space", None, None))
    return jax.shard_map(
        per_device, mesh=mesh, in_specs=in_specs, out_specs=out_specs, check_vma=False
    )
```

profile of v0, /device:TPU:12, one launch (start us, length us, event | category | flops | bytes accessed | tf_op | source)
XLA Modules:
  0.0 50.5 jit_solution(4857258129713414698)
XLA Ops:
  0.6 0.0 copy-start.4
  0.6 0.7 %reshape.21.coupling = f32[1,1680]{1,0:T(1,128)S(1)} reshape(f32[1680]{0:T(1024)} %param.11) | data formatting | bytes 13440 | tf_op jit(solution)/shard_map/reshape | solution.py:459
  1.3 0.0 copy-done.4
  1.4 0.0 copy-start
  1.4 1.0 %copy-done = f32[60,2,8,128]{3,2,1,0:T(8,128)S(1)} copy-done((f32[60,2,8,128]{3,2,1,0:T(8,128)S(1)}, f32[60,2,8,128]{3,2,1,0:T(8,128)}, u32[]{:S(2)}) %copy-start) | copy-done | bytes 491544
  2.4 0.0 copy-start.1
  2.4 1.0 %copy-done.1 = f32[60,2,8,128]{3,2,1,0:T(8,128)S(1)} copy-done((f32[60,2,8,128]{3,2,1,0:T(8,128)S(1)}, f32[60,2,8,128]{3,2,1,0:T(8,128)}, u32[]{:S(2)}) %copy-start.1) | copy-done | bytes 491544
  3.4 0.0 copy-start.2
  3.4 0.8 %copy-done.2 = f32[7,2,8,128]{3,2,1,0:T(8,128)S(1)} copy-done((f32[7,2,8,128]{3,2,1,0:T(8,128)S(1)}, f32[7,2,8,128]{3,2,1,0:T(8,128)}, u32[]{:S(2)}) %copy-start.2) | copy-done | bytes 57368
  4.2 0.0 copy-start.3
  4.2 0.7 %copy-done.3 = s32[3,1680]{1,0:T(4,128)S(1)} copy-done((s32[3,1680]{1,0:T(4,128)S(1)}, s32[3,1680]{1,0:T(4,128)}, u32[]{:S(2)}) %copy-start.3) | copy-done | bytes 20184
  5.0 44.0 %shard_map.77 = (f32[960,128]{1,0:T(8,128)S(1)}, f32[960,128]{1,0:T(8,128)S(1)}) custom-call(f32[960,128]{1,0:T(8,128)S(1)} %bitcast.4, f32[960,128]{1,0:T(8,128)S(1)} %bitcast.5, f32[2,8,128]{2,1,0:T(8,128)S(1)} %copy-done.4, f32[7,2,8,128]{3,2,1,0:T(8,128)S(1)} %copy-done.2, s32[3,1680]{1,0:T(4,128)S(1)} %copy-done.3, f32[1,1680]{1,0:T(1,128)S(1)} %reshape.21.coupling), custom_call_target="tpu_custom_call" | custom-call | tf_op jit(solution)/shard_map/pallas_call | solution.py:419
  49.0 0.8 %copy.10 = f32[60,2,8,128]{3,2,1,0:T(8,128)} copy(f32[60,2,8,128]{3,2,1,0:T(8,128)S(1)} %bitcast.7) | data formatting | bytes 983040
  49.7 0.8 %copy.11 = f32[60,2,8,128]{3,2,1,0:T(8,128)} copy(f32[60,2,8,128]{3,2,1,0:T(8,128)S(1)} %bitcast.6) | data formatting | bytes 983040
Async XLA Ops:
  0.6 0.7 %copy-start.4 = (f32[2,8,128]{2,1,0:T(8,128)S(1)}, f32[2,8,128]{2,1,0:T(8,128)}, u32[]{:S(2)}) copy-start(f32[2,8,128]{2,1,0:T(8,128)} %mean.1) | copy-start | bytes 24580
  1.4 1.0 %copy-start = (f32[60,2,8,128]{3,2,1,0:T(8,128)S(1)}, f32[60,2,8,128]{3,2,1,0:T(8,128)}, u32[]{:S(2)}) copy-start(f32[60,2,8,128]{3,2,1,0:T(8,128)} %param.6) | copy-start | bytes 1474564
  2.4 1.0 %copy-start.1 = (f32[60,2,8,128]{3,2,1,0:T(8,128)S(1)}, f32[60,2,8,128]{3,2,1,0:T(8,128)}, u32[]{:S(2)}) copy-start(f32[60,2,8,128]{3,2,1,0:T(8,128)} %param.7) | copy-start | bytes 1474564
  3.4 0.8 %copy-start.2 = (f32[7,2,8,128]{3,2,1,0:T(8,128)S(1)}, f32[7,2,8,128]{3,2,1,0:T(8,128)}, u32[]{:S(2)}) copy-start(f32[7,2,8,128]{3,2,1,0:T(8,128)} %fluct.1) | copy-start | bytes 172036
  4.2 0.7 %copy-start.3 = (s32[3,1680]{1,0:T(4,128)S(1)}, s32[3,1680]{1,0:T(4,128)}, u32[]{:S(2)}) copy-start(s32[3,1680]{1,0:T(4,128)} %triples.1) | copy-start | bytes 60484
where the time goes:
time: 50.9 us; the launch traced here: 50.5 us
  Pallas kernels  44 us (86%)
  local copies, waits for them, and re-layouts  5.89 us (12%)
  between operations  0.66 us (1%)
    pallas_call x1, Pallas kernels, per_device(): pl.pallas_call(functools.partial(kernel, dims), out_shape=(flat, flat), i...  44 us
    unnamed x12, local copies, waits for them, and re-layouts  5.18 us

commit v1 on v0

--- a/solution.py
+++ b/solution.py
@@ -13,12 +13,15 @@
 ROWS = 32
 
 
-def kernel(dims, guess, source, mean, fluct, triples, coupling, sol_out, upd_out,
+def kernel(dims, guess_in, source_in, mean_in, fluct_in, triples_in, coupling_in, sol_out, upd_out,
+           guess, source, triples, coupling, in_sem,
            field, rhs, pack_g, pack_s, back_s, back_u, last, coef, tile, faces, inverse,
            pattern, table, fine, coarse, plain,
            coef_sem, guess_sem, rhs_sem, rim_sem, x_sem, y_sem, sol_sem, upd_sem):
     slabs, groups, blocks, room, planes, rows, depth, terms, entries = dims
     share = rows // groups
+    band = 2 if share % 2 == 0 else 1
+    bands = share // band
     width = room * groups
     f32, bf16 = jnp.float32, jnp.bfloat16
     here = lax.axis_index("space")
@@ -41,6 +44,17 @@
     def plane_at(q):
         return jnp.where(even, planes - 1 - q, q)
 
+    inputs = [
+        pltpu.make_async_copy(guess_in, guess, in_sem.at[0]),
+        pltpu.make_async_copy(mean_in, coef.at[0, pl.ds(1, planes)], in_sem.at[1]),
+        pltpu.make_async_copy(fluct_in, coef.at[pl.ds(1, terms - 1), pl.ds(1, planes)], in_sem.at[2]),
+        pltpu.make_async_copy(source_in, source, in_sem.at[3]),
+        pltpu.make_async_copy(triples_in, triples, in_sem.at[4]),
+        pltpu.make_async_copy(coupling_in, coupling, in_sem.at[5]),
+    ]
+    for copy in inputs:
+        copy.start()
+
     @pl.when(here == 0)
     def _():
         field[:, 0] = jnp.zeros((ITERS, share + 2, width, depth), f32)
@@ -83,24 +97,9 @@
         part = ref[pl.ds(p * rows + y, blocks, stride=planes * rows), :]
         return jnp.concatenate([part, gap], axis=0) if room > blocks else part
 
-    for t in range(groups):
-        for p in range(planes):
-            for r in range(share + 2):
-                y = t * share + r - 1
-                if 0 <= y < rows:
-                    pack_g[t, p, r] = rows_of(guess, p, y)
-                elif groups != 2:
-                    pack_g[t, p, r] = jnp.zeros((room, depth), f32)
-
-    pl.semaphore_wait(barrier, groups - 1 + has_prev.astype(jnp.int32) + has_next.astype(jnp.int32))
-
-    def coef_copies(up):
-        at, to, space = (planes - 1, 0, here + 1) if up else (0, planes + 1, here - 1)
-        way = 0 if up else 1
-        return [
-            remote(mean.at[at], coef.at[0, to], coef_sem, (way, 0), space, me),
-            remote(fluct.at[:, at], coef.at[pl.ds(1, terms - 1), to], coef_sem, (way, 1), space, me),
-        ]
+    def coef_copy(up):
+        at, to, space = (planes, 0, here + 1) if up else (1, planes + 1, here - 1)
+        return remote(coef.at[:, at], coef.at[:, to], coef_sem, (0 if up else 1,), space, me)
 
     def guess_copy(d, p, owner, target):
         start = first_row(target)
@@ -109,20 +108,35 @@
             field.at[0, p + 1, pl.ds(start, tall), block(owner)],
             guess_sem, (d, p), here, target)
 
+    def guess_row(p, target, at):
+        y = target * share + at - 1
+        inside = jnp.clip(y, 0, rows - 1)
+        part = rows_of(guess, p, inside)
+        return part if groups == 2 else jnp.where(y == inside, part, 0.0)
+
+    inputs[0].wait()
     for q in range(planes):
         p = plane_at(planes - 1 - q)
         for d in range(1, groups):
-            guess_copy(d, p, me, group(d)).start()
+            target = group(d)
+            for r in range(tall):
+                at = first_row(target) + r
+                pack_g[target, p, at] = guess_row(p, target, at)
+            if q == 0 and d == 1:
+                pl.semaphore_wait(
+                    barrier, groups - 1 + has_prev.astype(jnp.int32) + has_next.astype(jnp.int32))
+            guess_copy(d, p, me, target).start()
+
+    inputs[1].wait()
+    inputs[2].wait()
 
     @pl.when(has_next)
     def _():
-        for copy in coef_copies(True):
-            copy.start()
+        coef_copy(True).start()
 
     @pl.when(has_prev)
     def _():
-        for copy in coef_copies(False):
-            copy.start()
+        coef_copy(False).start()
 
     def rim_copy(up, d, owner):
         at, to, space = (planes, 0, here + 1) if up else (1, planes + 1, here - 1)
@@ -133,7 +147,7 @@
     for p in range(planes):
         for r in range(tall):
             at = first_row(me) + r
-            field[0, p + 1, at, block(me)] = pack_g[me, p, at]
+            field[0, p + 1, at, block(me)] = guess_row(p, me, at)
 
     @pl.when(has_next)
     def _():
@@ -143,12 +157,19 @@
     def _():
         rim_copy(False, 0, me).start()
 
-    for t in range(groups):
+    inputs[3].wait()
+    for d in range(groups):
+        target = group(d)
         for p in range(planes):
             for r in range(share):
-                pack_s[t, p, r] = rows_of(source, p, t * share + r)
-    rhs[:, :, block(me)] = pack_s[me]
-
+                part = rows_of(source, p, target * share + r)
+                if d == 0:
+                    rhs[p, r, block(me)] = part
+                else:
+                    pack_s[target, p, r] = part
+
+    inputs[4].wait()
+    inputs[5].wait()
     pattern[...] = jnp.full(pattern.shape, -1, jnp.int32)
     pattern[0:3, 0:entries] = triples[...]
     length = pattern.shape[1]
@@ -161,7 +182,7 @@
 
     owner_row = spread(pattern[0:1, :])
     column = spread(pattern[1:2, :]) + (pattern[2:3, :] - 1) * width
-    value = jnp.concatenate([coupling[...], jnp.zeros((1, length - entries), f32)], axis=1)
+    value = jnp.concatenate([coupling[...].reshape(1, entries), jnp.zeros((1, length - entries), f32)], axis=1)
     high = value.astype(bf16).astype(f32)
     low = value - high
     hit = lax.broadcasted_iota(jnp.int32, (width, length), 0) == owner_row
@@ -180,34 +201,30 @@
     def rhs_copy(d, owner, target):
         return remote(pack_s.at[target], rhs.at[:, :, block(owner)], rhs_sem, (d,), here, target)
 
-    for d in range(1, groups):
-        owner = group(-d)
-        for p in range(planes):
+    for q in range(planes):
+        p = plane_at(planes - 1 - q)
+        for d in range(1, groups):
+            owner = group(-d)
             guess_copy(d, p, owner, me).wait_recv()
 
-        @pl.when(has_next)
-        def _():
-            rim_copy(True, d, owner).start()
-
-        @pl.when(has_prev)
-        def _():
-            rim_copy(False, d, owner).start()
+            @pl.when((p == planes - 1) & has_next)
+            def _():
+                rim_copy(True, d, owner).start()
+
+            @pl.when((p == 0) & has_prev)
+            def _():
+                rim_copy(False, d, owner).start()
 
     for d in range(1, groups):
         rhs_copy(d, me, group(d)).start()
 
-    coef[0, 1:planes + 1] = mean[...]
-    coef[1:, 1:planes + 1] = fluct[...]
-
     @pl.when(has_prev)
     def _():
-        for copy in coef_copies(True):
-            copy.wait_recv()
+        coef_copy(True).wait_recv()
 
     @pl.when(has_next)
     def _():
-        for copy in coef_copies(False):
-            copy.wait_recv()
+        coef_copy(False).wait_recv()
 
     def face_step(k, p):
         a = coef[k, p + 1]
@@ -238,9 +255,10 @@
 
     lane = lax.broadcasted_iota(jnp.int32, (ROWS, depth), 1)
 
-    def gather_terms(step, p):
+    def gather_terms(step, p, base):
         def by_block(index, carry):
-            r = index // (width // ROWS)
+            line = index // (width // ROWS)
+            r = base + line
             begin = pl.multiple_of(lax.rem(index, width // ROWS) * ROWS, ROWS)
 
             def cells(a, b):
@@ -259,22 +277,22 @@
                     acc = acc + faces[p, r, k, n][None] * drops[n]
                 acc = acc.reshape(ROWS, depth)
                 if k == 0:
-                    plain[r, pl.ds(begin, ROWS), :] = acc
+                    plain[line, pl.ds(begin, ROWS), :] = acc
                 else:
                     top = acc.astype(bf16)
                     at = pl.ds(pl.multiple_of((k - 1) * width + begin, ROWS), ROWS)
-                    lanes = pl.ds(pl.multiple_of(r * depth, depth), depth)
+                    lanes = pl.ds(pl.multiple_of(line * depth, depth), depth)
                     coarse[at, lanes] = top
                     fine[at, lanes] = (acc - top.astype(f32)).astype(bf16)
             return carry
 
-        lax.fori_loop(0, share * (width // ROWS), by_block, 0)
-
-    def x_copy(step, up):
+        lax.fori_loop(0, band * (width // ROWS), by_block, 0)
+
+    def x_copy(step, up, part):
         at, to, space = (planes, 0, here + 1) if up else (1, planes + 1, here - 1)
-        span = pl.ds(1, share)
+        span = pl.ds(1 + part * band, band)
         return remote(field.at[step, at, span], field.at[step, to, span],
-                      x_sem, (step, 0 if up else 1), space, me)
+                      x_sem, (step, 0 if up else 1, part), space, me)
 
     def y_copy(step, p, right):
         at, to, mode = (share, 0, me + 1) if right else (1, share + 1, me - 1)
@@ -285,50 +303,66 @@
         return remote(field.at[ITERS - 1, p + 1, pl.ds(1, share), block(target)], back_s.at[slot, p],
                       sol_sem, (d, p), here, target)
 
-    def upd_copy(d, p, slot, target):
-        return remote(last.at[p, :, block(target)], back_u.at[slot, p], upd_sem, (d, p), here, target)
-
-    def await_rims(step, p):
+    def upd_copy(d, p, part, slot, target):
+        span = pl.ds(part * band, band)
+        return remote(last.at[p, span, block(target)], back_u.at[slot, p, span],
+                      upd_sem, (d, p, part), here, target)
+
+    def await_rims(step, p, part):
+        first = part == 0
+
         @pl.when((p == 0) & has_prev)
         def _():
             if step == 0:
-                for d in range(groups):
-                    rim_copy(True, d, group(-d)).wait_recv()
+                @pl.when(first)
+                def _():
+                    for d in range(groups):
+                        rim_copy(True, d, group(-d)).wait_recv()
             else:
-                x_copy(step, True).wait_recv()
+                x_copy(step, True, part).wait_recv()
 
         @pl.when((p == planes - 1) & has_next)
         def _():
             if step == 0:
-                for d in range(groups):
-                    rim_copy(False, d, group(-d)).wait_recv()
+                @pl.when(first)
+                def _():
+                    for d in range(groups):
+                        rim_copy(False, d, group(-d)).wait_recv()
             else:
-                x_copy(step, False).wait_recv()
+                x_copy(step, False, part).wait_recv()
 
         if step > 0:
-            @pl.when(has_left)
+            @pl.when(has_left & first)
             def _():
                 y_copy(step, p, True).wait_recv()
 
-            @pl.when(has_right)
+            @pl.when(has_right & (part == bands - 1))
             def _():
                 y_copy(step, p, False).wait_recv()
 
     for step in range(ITERS):
-        def sweep(q, carry, step=step):
+        def sweep(unit, carry, step=step):
+            q, part = unit // bands, lax.rem(unit, bands)
             p = plane_at(q)
-            await_rims(step, p)
-            gather_terms(step, p)
+            base = part * band
+            await_rims(step, p, part)
+            if step == ITERS - 1:
+                @pl.when(unit == planes * bands - 1)
+                def _():
+                    for d in range(1, groups):
+                        sol_copy(d, p, me, group(d)).start()
+            gather_terms(step, p, base)
             both = jnp.dot(table[...], coarse[...], preferred_element_type=f32)
             image = both[:width] + both[width:]
             image = image + jnp.dot(table[:width], fine[...], preferred_element_type=f32)
             if step == 0:
-                @pl.when(q == 0)
+                @pl.when(unit == 0)
                 def _():
                     for d in range(1, groups):
                         rhs_copy(d, group(-d), me).wait_recv()
-            for r in range(share):
-                rest = rhs[p, r] - plain[r] - image[:, r * depth:(r + 1) * depth]
+            for line in range(band):
+                r = base + line
+                rest = rhs[p, r] - plain[line] - image[:, line * depth:(line + 1) * depth]
                 rest = rest.reshape(width // SUB, SUB, depth) * inverse[p, r][None]
                 rest = rest.reshape(width, depth)
                 if step < ITERS - 1:
@@ -338,60 +372,67 @@
             if step < ITERS - 1:
                 @pl.when((p == planes - 1) & has_next)
                 def _():
-                    x_copy(step + 1, True).start()
+                    x_copy(step + 1, True, part).start()
 
                 @pl.when((p == 0) & has_prev)
                 def _():
-                    x_copy(step + 1, False).start()
-
-                @pl.when(has_right)
+                    x_copy(step + 1, False, part).start()
+
+                @pl.when(has_right & (part == bands - 1))
                 def _():
                     y_copy(step + 1, p, True).start()
 
-                @pl.when(has_left)
+                @pl.when(has_left & (part == 0))
                 def _():
                     y_copy(step + 1, p, False).start()
 
             if step == ITERS - 2:
-                for d in range(1, groups):
-                    sol_copy(d, p, me, group(d)).start()
+                @pl.when((part == bands - 1) & (q < planes - 1))
+                def _():
+                    for d in range(1, groups):
+                        sol_copy(d, p, me, group(d)).start()
             if step == ITERS - 1:
                 for d in range(1, groups):
-                    upd_copy(d, p, me, group(d)).start()
+                    upd_copy(d, p, part, me, group(d)).start()
             return carry
 
-        lax.fori_loop(0, planes, sweep, 0)
+        lax.fori_loop(0, planes * bands, sweep, 0)
+
+    def write(p, g, lines, base, change, start):
+        for r in range(lines):
+            at = pl.ds(p * rows + g * share + base + r, blocks, stride=planes * rows)
+            upd_out[at, :] = change[r][:blocks]
+            sol_out[at, :] = start[r][:blocks] + 0.5 * change[r][:blocks]
 
     for p in range(planes):
-        back_s[me, p] = field[ITERS - 1, p + 1, 1:share + 1, block(me)]
-        back_u[me, p] = last[p, :, block(me)]
-    for d in range(1, groups):
-        for p in range(planes):
-            sol_copy(d, p, group(-d), me).wait_recv()
-            upd_copy(d, p, group(-d), me).wait_recv()
-    for g in range(groups):
-        for p in range(planes):
-            for r in range(share):
-                at = pl.ds(p * rows + g * share + r, blocks, stride=planes * rows)
-                change = back_u[g, p, r][:blocks]
-                upd_out[at, :] = change
-                sol_out[at, :] = back_s[g, p, r][:blocks] + 0.5 * change
+        write(p, me, share, 0, last[p, :, block(me)],
+              field[ITERS - 1, p + 1, 1:share + 1, block(me)])
+    for q in range(planes):
+        p = plane_at(q)
+        for d in range(1, groups):
+            g = group(-d)
+            sol_copy(d, p, g, me).wait_recv()
+            for part in range(bands):
+                upd_copy(d, p, part, g, me).wait_recv()
+                span = pl.ds(part * band, band)
+                write(p, g, band, part * band, back_u[g, p, span], back_s[g, p, span])
 
     for d in range(1, groups):
         for p in range(planes):
             guess_copy(d, p, me, group(d)).wait_send()
             sol_copy(d, p, me, group(d)).wait_send()
-            upd_copy(d, p, me, group(d)).wait_send()
+            for part in range(bands):
+                upd_copy(d, p, part, me, group(d)).wait_send()
         rhs_copy(d, me, group(d)).wait_send()
     for up, has in ((True, has_next), (False, has_prev)):
         @pl.when(has)
         def _():
-            for copy in coef_copies(up):
-                copy.wait_send()
+            coef_copy(up).wait_send()
             for d in range(groups):
                 rim_copy(up, d, group(-d)).wait_send()
             for step in range(1, ITERS):
-                x_copy(step, up).wait_send()
+                for part in range(bands):
+                    x_copy(step, up, part).wait_send()
     for right, has in ((True, has_right), (False, has_left)):
         @pl.when(has)
         def _():
@@ -406,6 +447,7 @@
     terms = fluct_coef.shape[0] + 1
     entries = triples.shape[1]
     share = rows // groups
+    band = 2 if share % 2 == 0 else 1
     room = -(-blocks // 16) * 16
     while (room * groups) % 128:
         room += 16
@@ -419,9 +461,14 @@
     solution, update = pl.pallas_call(
         functools.partial(kernel, dims),
         out_shape=(flat, flat),
-        in_specs=[vmem] * 6,
+        in_specs=[pl.BlockSpec(memory_space=pltpu.HBM)] * 6,
         out_specs=(vmem, vmem),
         scratch_shapes=[
+            pltpu.VMEM(flat.shape, f32),
+            pltpu.VMEM(flat.shape, f32),
+            pltpu.VMEM(triples.shape, jnp.int32),
+            pltpu.VMEM(coupling.shape, f32),
+            dma((6,)),
             pltpu.VMEM((ITERS, planes + 2, share + 2, width, depth), f32),
             pltpu.VMEM((planes, share, width, depth), f32),
             pltpu.VMEM((groups, planes, share + 2, room, depth), f32),
@@ -435,20 +482,20 @@
             pltpu.VMEM((planes, share, SUB, depth), f32),
             pltpu.VMEM((SUB, length), jnp.int32),
             pltpu.VMEM((2 * width, (terms - 1) * width), bf16),
-            pltpu.VMEM(((terms - 1) * width, share * depth), bf16),
-            pltpu.VMEM(((terms - 1) * width, share * depth), bf16),
-            pltpu.VMEM((share, width, depth), f32),
-            dma((2, 2, 2)),
+            pltpu.VMEM(((terms - 1) * width, band * depth), bf16),
+            pltpu.VMEM(((terms - 1) * width, band * depth), bf16),
+            pltpu.VMEM((band, width, depth), f32),
+            dma((2, 2)),
             dma((2, groups, planes)),
             dma((2, groups)),
             dma((2, 2, groups)),
-            dma((2, ITERS, 2)),
+            dma((2, ITERS, 2, share // band)),
             dma((2, ITERS, 2, planes)),
             dma((2, groups, planes)),
-            dma((2, groups, planes)),
+            dma((2, groups, planes, share // band)),
         ],
         compiler_params=pltpu.CompilerParams(
-            collective_id=0, has_side_effects=True, vmem_limit_bytes=48 * 1024 * 1024
+            collective_id=0, has_side_effects=True, vmem_limit_bytes=62 * 1024 * 1024
         ),
     )(
         guess.reshape(flat.shape),
@@ -456,7 +503,7 @@
         mean_coef,
         fluct_coef,
         triples,
-        coupling.reshape(1, entries),
+        coupling,
     )
     return solution.reshape(guess.shape), update.reshape(guess.shape)
 

time: 50.9 us -> 47.1 us (0.925)
  the two profiles are of different devices: /device:TPU:12 before, /device:TPU:0 now
where the time goes in v1:
time: 47.1 us; the launch traced here: 47 us
  Pallas kernels  43.7 us (93%)
  local copies, waits for them, and re-layouts  2.68 us (6%)
  between operations  0.65 us (1%)
    pallas_call x1, Pallas kernels, per_device(): pl.pallas_call(functools.partial(kernel, dims), out_shape=(flat, flat), i...  43.7 us
    unnamed x4, local copies, waits for them, and re-layouts  2.68 us

profile of v1, /device:TPU:0, one launch (start us, length us, event | category | flops | bytes accessed | tf_op | source)
XLA Modules:
  0.0 47.0 jit_solution(2153110278623101915)
XLA Ops:
  0.6 43.7 %shard_map.77 = (f32[960,128]{1,0:T(8,128)}, f32[960,128]{1,0:T(8,128)}) custom-call(f32[960,128]{1,0:T(8,128)} %bitcast.4, f32[960,128]{1,0:T(8,128)} %bitcast.5, f32[2,8,128]{2,1,0:T(8,128)} %mean_in.1, f32[7,2,8,128]{3,2,1,0:T(8,128)} %fluct_in.1, s32[3,1680]{1,0:T(4,128)} %triples_in.1, f32[1680]{0:T(1024)} %coupling_in.1), custom_call_target="tpu_custom_call" | custom-call | tf_op jit(solution)/shard_map/pallas_call | solution.py:461
  44.3 0.0 copy-start
  44.3 1.9 %copy.10 = f32[60,2,8,128]{3,2,1,0:T(8,128)} copy(f32[60,2,8,128]{3,2,1,0:T(8,128)} %bitcast.7) | data formatting | bytes 983040
  46.2 0.0 copy-done
  46.2 0.8 %copy.11 = f32[60,2,8,128]{3,2,1,0:T(8,128)} copy(f32[60,2,8,128]{3,2,1,0:T(8,128)S(1)} %bitcast.6) | data formatting | bytes 983040
Async XLA Ops:
  44.3 1.9 %copy-start = (f32[960,128]{1,0:T(8,128)S(1)}, f32[960,128]{1,0:T(8,128)}, u32[]{:S(2)}) copy-start(f32[960,128]{1,0:T(8,128)} %get-tuple-element.5) | copy-start | bytes 1474564

commit v2 on v1

--- a/solution.py
+++ b/solution.py
@@ -13,10 +13,10 @@
 ROWS = 32
 
 
-def kernel(dims, guess_in, source_in, mean_in, fluct_in, triples_in, coupling_in, sol_out, upd_out,
+def kernel(dims, guess_in, source_in, mean_in, fluct_in, triples_in, coupling_in, sol_out, rest_out, diagonal,
            guess, source, triples, coupling, in_sem,
            field, rhs, pack_g, pack_s, back_s, back_u, last, coef, tile, faces, inverse,
-           pattern, table, fine, coarse, plain,
+           pattern, table, plain,
            coef_sem, guess_sem, rhs_sem, rim_sem, x_sem, y_sem, sol_sem, upd_sem):
     slabs, groups, blocks, room, planes, rows, depth, terms, entries = dims
     share = rows // groups
@@ -181,42 +181,23 @@
         return i + shift
 
     owner_row = spread(pattern[0:1, :])
-    column = spread(pattern[1:2, :]) + (pattern[2:3, :] - 1) * width
+    partner = spread(pattern[1:2, :])
+    chunk = (terms - 1) * ROWS
+    column = partner + (partner // ROWS) * (chunk - ROWS) + (pattern[2:3, :] - 1) * ROWS
     value = jnp.concatenate([coupling[...].reshape(1, entries), jnp.zeros((1, length - entries), f32)], axis=1)
     high = value.astype(bf16).astype(f32)
     low = value - high
     hit = lax.broadcasted_iota(jnp.int32, (width, length), 0) == owner_row
     picks = jnp.concatenate(
         [jnp.where(hit, high, 0.0).astype(bf16), jnp.where(hit, low, 0.0).astype(bf16)], axis=0)
-
-    for k in range(terms - 1):
-        chosen = lax.broadcasted_iota(jnp.int32, (width, length), 0) + k * width == column
-        chosen = jnp.where(chosen, 1.0, 0.0).astype(bf16)
+    order = lax.broadcasted_iota(jnp.int32, (chunk, length), 0)
+    for b in range(width // ROWS):
+        chosen = jnp.where(order == column - b * chunk, 1.0, 0.0).astype(bf16)
         both = lax.dot_general(picks, chosen, (((1,), (1,)), ((), ())), preferred_element_type=f32)
         entry = both[:width] + both[width:]
         top = entry.astype(bf16)
-        table[:width, k * width:(k + 1) * width] = top
-        table[width:, k * width:(k + 1) * width] = (entry - top.astype(f32)).astype(bf16)
-
-    def rhs_copy(d, owner, target):
-        return remote(pack_s.at[target], rhs.at[:, :, block(owner)], rhs_sem, (d,), here, target)
-
-    for q in range(planes):
-        p = plane_at(planes - 1 - q)
-        for d in range(1, groups):
-            owner = group(-d)
-            guess_copy(d, p, owner, me).wait_recv()
-
-            @pl.when((p == planes - 1) & has_next)
-            def _():
-                rim_copy(True, d, owner).start()
-
-            @pl.when((p == 0) & has_prev)
-            def _():
-                rim_copy(False, d, owner).start()
-
-    for d in range(1, groups):
-        rhs_copy(d, me, group(d)).start()
+        table[b, :width, :] = top
+        table[b, width:, :] = (entry - top.astype(f32)).astype(bf16)
 
     @pl.when(has_prev)
     def _():
@@ -236,6 +217,14 @@
         tile[3] = 0.5 * (a + jnp.where(row == 0, 0.0, pltpu.roll(a, 1, 0)))
         tile[4] = 0.5 * (a + jnp.where(lane == depth - 1, 0.0, pltpu.roll(a, depth - 1, 1)))
         tile[5] = 0.5 * (a + jnp.where(lane == 0, 0.0, pltpu.roll(a, 1, 1)))
+
+        @pl.when(k == 0)
+        def _():
+            total = tile[0]
+            for n in range(1, 6):
+                total = total + tile[n]
+            diagonal[p] = total
+
         for r in range(share):
             for n in range(6):
                 faces[p, r, k, n] = jnp.broadcast_to(tile[n, pl.ds(me * share + r, 1), :], (SUB, depth))
@@ -253,40 +242,67 @@
                 total = total + faces[p, r, 0, n]
             inverse[p, r] = 1.0 / total
 
+    def rhs_copy(d, owner, target):
+        return remote(pack_s.at[target], rhs.at[:, :, block(owner)], rhs_sem, (d,), here, target)
+
+    for q in range(planes):
+        p = plane_at(planes - 1 - q)
+        for d in range(1, groups):
+            owner = group(-d)
+            guess_copy(d, p, owner, me).wait_recv()
+
+            @pl.when((p == planes - 1) & has_next)
+            def _():
+                rim_copy(True, d, owner).start()
+
+            @pl.when((p == 0) & has_prev)
+            def _():
+                rim_copy(False, d, owner).start()
+
+    for d in range(1, groups):
+        rhs_copy(d, me, group(d)).start()
+
     lane = lax.broadcasted_iota(jnp.int32, (ROWS, depth), 1)
 
-    def gather_terms(step, p, base):
-        def by_block(index, carry):
-            line = index // (width // ROWS)
-            r = base + line
-            begin = pl.multiple_of(lax.rem(index, width // ROWS) * ROWS, ROWS)
-
-            def cells(a, b):
-                return field[step, a, b, pl.ds(begin, ROWS), :]
-
-            centre = cells(p + 1, r + 1)
-            others = [
-                cells(p + 2, r + 1), cells(p, r + 1), cells(p + 1, r + 2), cells(p + 1, r),
-                jnp.where(lane == depth - 1, 0.0, pltpu.roll(centre, depth - 1, 1)),
-                jnp.where(lane == 0, 0.0, pltpu.roll(centre, 1, 1)),
-            ]
-            drops = [(centre - other).reshape(ROWS // SUB, SUB, depth) for other in others]
-            for k in range(terms):
-                acc = faces[p, r, k, 0][None] * drops[0]
-                for n in range(1, 6):
-                    acc = acc + faces[p, r, k, n][None] * drops[n]
-                acc = acc.reshape(ROWS, depth)
-                if k == 0:
-                    plain[line, pl.ds(begin, ROWS), :] = acc
-                else:
-                    top = acc.astype(bf16)
-                    at = pl.ds(pl.multiple_of((k - 1) * width + begin, ROWS), ROWS)
-                    lanes = pl.ds(pl.multiple_of(line * depth, depth), depth)
-                    coarse[at, lanes] = top
-                    fine[at, lanes] = (acc - top.astype(f32)).astype(bf16)
-            return carry
-
-        lax.fori_loop(0, band * (width // ROWS), by_block, 0)
+    def mix(step, p, base):
+        image = jnp.zeros((width, band * depth), f32)
+        second = jnp.zeros((width, band * depth), f32)
+        for b in range(width // ROWS):
+            begin = b * ROWS
+            tops, rests = [], []
+            for line in range(band):
+                r = base + line
+
+                def cells(x, y):
+                    return field[step, x, y, begin:begin + ROWS, :]
+
+                centre = cells(p + 1, r + 1)
+                others = [
+                    cells(p + 2, r + 1), cells(p, r + 1), cells(p + 1, r + 2), cells(p + 1, r),
+                    jnp.where(lane == depth - 1, 0.0, pltpu.roll(centre, depth - 1, 1)),
+                    jnp.where(lane == 0, 0.0, pltpu.roll(centre, 1, 1)),
+                ]
+                drops = [(centre - other).reshape(ROWS // SUB, SUB, depth) for other in others]
+                highs, lows = [], []
+                for k in range(terms):
+                    acc = faces[p, r, k, 0][None] * drops[0]
+                    for n in range(1, 6):
+                        acc = acc + faces[p, r, k, n][None] * drops[n]
+                    acc = acc.reshape(ROWS, depth)
+                    if k == 0:
+                        plain[line, begin:begin + ROWS, :] = acc
+                    else:
+                        top = acc.astype(bf16)
+                        highs.append(top)
+                        lows.append((acc - top.astype(f32)).astype(bf16))
+                tops.append(jnp.concatenate(highs, axis=0))
+                rests.append(jnp.concatenate(lows, axis=0))
+            coarse = jnp.concatenate(tops, axis=1)
+            fine = jnp.concatenate(rests, axis=1)
+            both = jnp.dot(table[b], coarse, preferred_element_type=f32)
+            image = image + both[:width] + jnp.dot(table[b, :width], fine, preferred_element_type=f32)
+            second = second + both[width:]
+        return image + second
 
     def x_copy(step, up, part):
         at, to, space = (planes, 0, here + 1) if up else (1, planes + 1, here - 1)
@@ -351,10 +367,7 @@
                 def _():
                     for d in range(1, groups):
                         sol_copy(d, p, me, group(d)).start()
-            gather_terms(step, p, base)
-            both = jnp.dot(table[...], coarse[...], preferred_element_type=f32)
-            image = both[:width] + both[width:]
-            image = image + jnp.dot(table[:width], fine[...], preferred_element_type=f32)
+            image = mix(step, p, base)
             if step == 0:
                 @pl.when(unit == 0)
                 def _():
@@ -363,9 +376,9 @@
             for line in range(band):
                 r = base + line
                 rest = rhs[p, r] - plain[line] - image[:, line * depth:(line + 1) * depth]
-                rest = rest.reshape(width // SUB, SUB, depth) * inverse[p, r][None]
-                rest = rest.reshape(width, depth)
                 if step < ITERS - 1:
+                    rest = rest.reshape(width // SUB, SUB, depth) * inverse[p, r][None]
+                    rest = rest.reshape(width, depth)
                     field[step + 1, p + 1, r + 1] = field[step, p + 1, r + 1] + 0.5 * rest
                 else:
                     last[p, r] = rest
@@ -398,24 +411,27 @@
 
         lax.fori_loop(0, planes * bands, sweep, 0)
 
-    def write(p, g, lines, base, change, start):
+    def write(out, p, g, lines, base, cells):
         for r in range(lines):
             at = pl.ds(p * rows + g * share + base + r, blocks, stride=planes * rows)
-            upd_out[at, :] = change[r][:blocks]
-            sol_out[at, :] = start[r][:blocks] + 0.5 * change[r][:blocks]
+            out[at, :] = cells[r][:blocks]
 
     for p in range(planes):
-        write(p, me, share, 0, last[p, :, block(me)],
-              field[ITERS - 1, p + 1, 1:share + 1, block(me)])
+        write(rest_out, p, me, share, 0, last[p, :, block(me)])
+        write(sol_out, p, me, share, 0, field[ITERS - 1, p + 1, 1:share + 1, block(me)])
     for q in range(planes):
         p = plane_at(q)
         for d in range(1, groups):
             g = group(-d)
             sol_copy(d, p, g, me).wait_recv()
+            write(sol_out, p, g, share, 0, back_s[g, p])
+    for q in range(planes):
+        p = plane_at(q)
+        for d in range(1, groups):
+            g = group(-d)
             for part in range(bands):
                 upd_copy(d, p, part, g, me).wait_recv()
-                span = pl.ds(part * band, band)
-                write(p, g, band, part * band, back_u[g, p, span], back_s[g, p, span])
+                write(rest_out, p, g, band, part * band, back_u[g, p, pl.ds(part * band, band)])
 
     for d in range(1, groups):
         for p in range(planes):
@@ -458,11 +474,11 @@
     flat = jax.ShapeDtypeStruct((blocks * planes * rows, depth), f32)
     dma = pltpu.SemaphoreType.DMA
     vmem = pl.BlockSpec(memory_space=pltpu.VMEM)
-    solution, update = pl.pallas_call(
+    base, rest, diagonal = pl.pallas_call(
         functools.partial(kernel, dims),
-        out_shape=(flat, flat),
+        out_shape=(flat, flat, jax.ShapeDtypeStruct((planes, rows, depth), f32)),
         in_specs=[pl.BlockSpec(memory_space=pltpu.HBM)] * 6,
-        out_specs=(vmem, vmem),
+        out_specs=(vmem, vmem, vmem),
         scratch_shapes=[
             pltpu.VMEM(flat.shape, f32),
             pltpu.VMEM(flat.shape, f32),
@@ -481,9 +497,7 @@
             pltpu.VMEM((planes, share, terms, 6, SUB, depth), f32),
             pltpu.VMEM((planes, share, SUB, depth), f32),
             pltpu.VMEM((SUB, length), jnp.int32),
-            pltpu.VMEM((2 * width, (terms - 1) * width), bf16),
-            pltpu.VMEM(((terms - 1) * width, band * depth), bf16),
-            pltpu.VMEM(((terms - 1) * width, band * depth), bf16),
+            pltpu.VMEM((width // ROWS, 2 * width, (terms - 1) * ROWS), bf16),
             pltpu.VMEM((band, width, depth), f32),
             dma((2, 2)),
             dma((2, groups, planes)),
@@ -505,7 +519,8 @@
         triples,
         coupling,
     )
-    return solution.reshape(guess.shape), update.reshape(guess.shape)
+    update = rest.reshape(guess.shape) / diagonal
+    return base.reshape(guess.shape) + 0.5 * update, update
 
 
 def solution(mesh):

time: 47.1 us -> 45 us (0.955)
  Pallas kernels: 43.7 us -> 41.3 us
  other arithmetic: 0 us -> 2.19 us
  local copies, waits for them, and re-layouts: 2.68 us -> 0.69 us
    pallas_call x1, Pallas kernels: 43.7 us -> 41.3 us  [per_device(): pl.pallas_call(functools.partial(kernel, dims), out_shape=(flat, flat, ja...]
    add x0 -> x1, other arithmetic: none -> 2.19 us  [per_device(): return (base.reshape(guess.shape) + 0.5 * update, update)]
    unnamed x4 -> x2, local copies, waits for them, and re-layouts: 2.68 us -> 0.69 us
where the time goes in v2:
time: 45 us; the launch traced here: 44.8 us
  Pallas kernels  41.3 us (92%)
  other arithmetic  2.19 us (5%)
  local copies, waits for them, and re-layouts  0.69 us (2%)
  between operations  0.65 us (1%)
    pallas_call x1, Pallas kernels, per_device(): pl.pallas_call(functools.partial(kernel, dims), out_shape=(flat, flat, ja...  41.3 us
    add x1, other arithmetic, per_device(): return (base.reshape(guess.shape) + 0.5 * update, update)  2.19 us

profile of v2, /device:TPU:0, one launch (start us, length us, event | category | flops | bytes accessed | tf_op | source)
XLA Modules:
  0.0 44.8 jit_solution(9686275530287741700)
XLA Ops:
  0.6 41.3 %shard_map.77 = (f32[960,128]{1,0:T(8,128)}, f32[960,128]{1,0:T(8,128)}, f32[2,8,128]{2,1,0:T(8,128)}) custom-call(f32[960,128]{1,0:T(8,128)} %bitcast.4, f32[960,128]{1,0:T(8,128)} %bitcast.5, f32[2,8,128]{2,1,0:T(8,128)} %mean_in.1, f32[7,2,8,128]{3,2,1,0:T(8,128)} %fluct_in.1, s32[3,1680]{1,0:T(4,128)} %triples_in.1, f32[1680]{0:T(1024)} %coupling_in.1), custom_call_target="tpu_custom_call" | custom-call | tf_op jit(solution)/shard_map/pallas_call | solution.py:477
  41.9 0.0 copy-start
  41.9 0.7 %copy-done = f32[2,8,128]{2,1,0:T(8,128)S(1)} copy-done((f32[2,8,128]{2,1,0:T(8,128)S(1)}, f32[2,8,128]{2,1,0:T(8,128)}, u32[]{:S(2)}) %copy-start) | copy-done | bytes 8216
  42.6 2.2 %multiply_add_fusion = (f32[60,2,8,128]{3,2,1,0:T(8,128)}, f32[60,2,8,128]{3,2,1,0:T(8,128)}) fusion(f32[60,2,8,128]{3,2,1,0:T(8,128)} %bitcast.6, f32[60,2,8,128]{3,2,1,0:T(8,128)} %bitcast.7, f32[2,8,128]{2,1,0:T(8,128)S(1)} %copy-done), kind=kLoop, calls=%fused_computation | loop fusion | flops 368640 | bytes 1974272 | tf_op jit(solution)/shard_map/add | solution.py:523
Async XLA Ops:
  41.9 0.7 %copy-start = (f32[2,8,128]{2,1,0:T(8,128)S(1)}, f32[2,8,128]{2,1,0:T(8,128)}, u32[]{:S(2)}) copy-start(f32[2,8,128]{2,1,0:T(8,128)} %get-tuple-element.7) | copy-start | bytes 24580

commit v3 on v2

--- a/solution.py
+++ b/solution.py
@@ -13,7 +13,7 @@
 ROWS = 32
 
 
-def kernel(dims, guess_in, source_in, mean_in, fluct_in, triples_in, coupling_in, sol_out, rest_out, diagonal,
+def kernel(dims, guess_in, source_in, mean_in, fluct_in, triples_in, coupling_in, sol_out, half_out,
            guess, source, triples, coupling, in_sem,
            field, rhs, pack_g, pack_s, back_s, back_u, last, coef, tile, faces, inverse,
            pattern, table, plain,
@@ -199,6 +199,12 @@
         table[b, :width, :] = top
         table[b, width:, :] = (entry - top.astype(f32)).astype(bf16)
 
+    def rhs_copy(d, owner, target):
+        return remote(pack_s.at[target], rhs.at[:, :, block(owner)], rhs_sem, (d,), here, target)
+
+    for d in range(1, groups):
+        rhs_copy(d, me, group(d)).start()
+
     @pl.when(has_prev)
     def _():
         coef_copy(True).wait_recv()
@@ -217,14 +223,6 @@
         tile[3] = 0.5 * (a + jnp.where(row == 0, 0.0, pltpu.roll(a, 1, 0)))
         tile[4] = 0.5 * (a + jnp.where(lane == depth - 1, 0.0, pltpu.roll(a, depth - 1, 1)))
         tile[5] = 0.5 * (a + jnp.where(lane == 0, 0.0, pltpu.roll(a, 1, 1)))
-
-        @pl.when(k == 0)
-        def _():
-            total = tile[0]
-            for n in range(1, 6):
-                total = total + tile[n]
-            diagonal[p] = total
-
         for r in range(share):
             for n in range(6):
                 faces[p, r, k, n] = jnp.broadcast_to(tile[n, pl.ds(me * share + r, 1), :], (SUB, depth))
@@ -242,9 +240,6 @@
                 total = total + faces[p, r, 0, n]
             inverse[p, r] = 1.0 / total
 
-    def rhs_copy(d, owner, target):
-        return remote(pack_s.at[target], rhs.at[:, :, block(owner)], rhs_sem, (d,), here, target)
-
     for q in range(planes):
         p = plane_at(planes - 1 - q)
         for d in range(1, groups):
@@ -259,8 +254,6 @@
             def _():
                 rim_copy(False, d, owner).start()
 
-    for d in range(1, groups):
-        rhs_copy(d, me, group(d)).start()
 
     lane = lax.broadcasted_iota(jnp.int32, (ROWS, depth), 1)
 
@@ -376,10 +369,10 @@
             for line in range(band):
                 r = base + line
                 rest = rhs[p, r] - plain[line] - image[:, line * depth:(line + 1) * depth]
+                rest = rest.reshape(width // SUB, SUB, depth) * (0.5 * inverse[p, r])[None]
+                rest = rest.reshape(width, depth)
                 if step < ITERS - 1:
-                    rest = rest.reshape(width // SUB, SUB, depth) * inverse[p, r][None]
-                    rest = rest.reshape(width, depth)
-                    field[step + 1, p + 1, r + 1] = field[step, p + 1, r + 1] + 0.5 * rest
+                    field[step + 1, p + 1, r + 1] = field[step, p + 1, r + 1] + rest
                 else:
                     last[p, r] = rest
             if step < ITERS - 1:
@@ -417,7 +410,7 @@
             out[at, :] = cells[r][:blocks]
 
     for p in range(planes):
-        write(rest_out, p, me, share, 0, last[p, :, block(me)])
+        write(half_out, p, me, share, 0, last[p, :, block(me)])
         write(sol_out, p, me, share, 0, field[ITERS - 1, p + 1, 1:share + 1, block(me)])
     for q in range(planes):
         p = plane_at(q)
@@ -431,7 +424,7 @@
             g = group(-d)
             for part in range(bands):
                 upd_copy(d, p, part, g, me).wait_recv()
-                write(rest_out, p, g, band, part * band, back_u[g, p, pl.ds(part * band, band)])
+                write(half_out, p, g, band, part * band, back_u[g, p, pl.ds(part * band, band)])
 
     for d in range(1, groups):
         for p in range(planes):
@@ -474,11 +467,11 @@
     flat = jax.ShapeDtypeStruct((blocks * planes * rows, depth), f32)
     dma = pltpu.SemaphoreType.DMA
     vmem = pl.BlockSpec(memory_space=pltpu.VMEM)
-    base, rest, diagonal = pl.pallas_call(
+    base, half = pl.pallas_call(
         functools.partial(kernel, dims),
-        out_shape=(flat, flat, jax.ShapeDtypeStruct((planes, rows, depth), f32)),
+        out_shape=(flat, flat),
         in_specs=[pl.BlockSpec(memory_space=pltpu.HBM)] * 6,
-        out_specs=(vmem, vmem, vmem),
+        out_specs=(vmem, vmem),
         scratch_shapes=[
             pltpu.VMEM(flat.shape, f32),
             pltpu.VMEM(flat.shape, f32),
@@ -519,8 +512,8 @@
         triples,
         coupling,
     )
-    update = rest.reshape(guess.shape) / diagonal
-    return base.reshape(guess.shape) + 0.5 * update, update
+    half = half.reshape(guess.shape)
+    return base.reshape(guess.shape) + half, 2.0 * half
 
 
 def solution(mesh):

time: 45 us -> 43.8 us (0.973)
  Pallas kernels: 41.3 us -> 40.6 us
  local copies, waits for them, and re-layouts: 0.69 us -> 0 us
    add x1 -> x0, other arithmetic: 2.19 us -> none  [per_device(): return (base.reshape(guess.shape) + 0.5 * update, update)]
    mul x0 -> x1, other arithmetic: none -> 2.18 us  [per_device(): return (base.reshape(guess.shape) + half, 2.0 * half)]
    unnamed x2 -> x0, local copies, waits for them, and re-layouts: 0.69 us -> none
    pallas_call x1, Pallas kernels: 41.3 us -> 40.6 us  [per_device(): pl.pallas_call(functools.partial(kernel, dims), out_shape=(flat, flat), i...]
where the time goes in v3:
time: 43.8 us; the launch traced here: 43.4 us
  Pallas kernels  40.6 us (93%)
  other arithmetic  2.18 us (5%)
  between operations  0.64 us (1%)
    pallas_call x1, Pallas kernels, per_device(): pl.pallas_call(functools.partial(kernel, dims), out_shape=(flat, flat), i...  40.6 us
    mul x1, other arithmetic, per_device(): return (base.reshape(guess.shape) + half, 2.0 * half)  2.18 us

profile of v3, /device:TPU:0, one launch (start us, length us, event | category | flops | bytes accessed | tf_op | source)
XLA Modules:
  0.0 43.4 jit_solution(16531397989682622777)
XLA Ops:
  0.6 40.6 %shard_map.77 = (f32[960,128]{1,0:T(8,128)}, f32[960,128]{1,0:T(8,128)}) custom-call(f32[960,128]{1,0:T(8,128)} %bitcast.4, f32[960,128]{1,0:T(8,128)} %bitcast.5, f32[2,8,128]{2,1,0:T(8,128)} %mean_in.1, f32[7,2,8,128]{3,2,1,0:T(8,128)} %fluct_in.1, s32[3,1680]{1,0:T(4,128)} %triples_in.1, f32[1680]{0:T(1024)} %coupling_in.1), custom_call_target="tpu_custom_call" | custom-call | tf_op jit(solution)/shard_map/pallas_call | solution.py:470
  41.2 2.2 %broadcast_multiply_fusion = (f32[960,128]{1,0:T(8,128)}, f32[960,128]{1,0:T(8,128)}) fusion(f32[960,128]{1,0:T(8,128)} %get-tuple-element.5, f32[960,128]{1,0:T(8,128)} %get-tuple-element.4), kind=kLoop, calls=%fused_computation | loop fusion | flops 245760 | bytes 1966080 | tf_op jit(solution)/shard_map/mul | solution.py:516

commit v4 on v3

--- a/solution.py
+++ b/solution.py
@@ -199,11 +199,12 @@
         table[b, :width, :] = top
         table[b, width:, :] = (entry - top.astype(f32)).astype(bf16)
 
-    def rhs_copy(d, owner, target):
-        return remote(pack_s.at[target], rhs.at[:, :, block(owner)], rhs_sem, (d,), here, target)
-
-    for d in range(1, groups):
-        rhs_copy(d, me, group(d)).start()
+    def rhs_copy(d, p, owner, target):
+        return remote(pack_s.at[target, p], rhs.at[p, :, block(owner)], rhs_sem, (d, p), here, target)
+
+    for q in range(planes):
+        for d in range(1, groups):
+            rhs_copy(d, plane_at(q), me, group(d)).start()
 
     @pl.when(has_prev)
     def _():
@@ -362,10 +363,10 @@
                         sol_copy(d, p, me, group(d)).start()
             image = mix(step, p, base)
             if step == 0:
-                @pl.when(unit == 0)
+                @pl.when(part == 0)
                 def _():
                     for d in range(1, groups):
-                        rhs_copy(d, group(-d), me).wait_recv()
+                        rhs_copy(d, p, group(-d), me).wait_recv()
             for line in range(band):
                 r = base + line
                 rest = rhs[p, r] - plain[line] - image[:, line * depth:(line + 1) * depth]
@@ -432,7 +433,7 @@
             sol_copy(d, p, me, group(d)).wait_send()
             for part in range(bands):
                 upd_copy(d, p, part, me, group(d)).wait_send()
-        rhs_copy(d, me, group(d)).wait_send()
+            rhs_copy(d, p, me, group(d)).wait_send()
     for up, has in ((True, has_next), (False, has_prev)):
         @pl.when(has)
         def _():
@@ -494,7 +495,7 @@
             pltpu.VMEM((band, width, depth), f32),
             dma((2, 2)),
             dma((2, groups, planes)),
-            dma((2, groups)),
+            dma((2, groups, planes)),
             dma((2, 2, groups)),
             dma((2, ITERS, 2, share // band)),
             dma((2, ITERS, 2, planes)),

time: 43.8 us -> 42.1 us (0.961)
  Pallas kernels: 40.6 us -> 38.8 us
    pallas_call x1, Pallas kernels: 40.6 us -> 38.8 us  [per_device(): pl.pallas_call(functools.partial(kernel, dims), out_shape=(flat, flat), i...]
where the time goes in v4:
time: 42.1 us; the launch traced here: 41.6 us
  Pallas kernels  38.8 us (92%)
  other arithmetic  2.18 us (5%)
  between operations  0.64 us (2%)
    pallas_call x1, Pallas kernels, per_device(): pl.pallas_call(functools.partial(kernel, dims), out_shape=(flat, flat), i...  38.8 us
    mul x1, other arithmetic, per_device(): return (base.reshape(guess.shape) + half, 2.0 * half)  2.18 us

profile of v4, /device:TPU:0, one launch (start us, length us, event | category | flops | bytes accessed | tf_op | source)
XLA Modules:
  0.0 41.6 jit_solution(5920380999867190338)
XLA Ops:
  0.6 38.8 %shard_map.77 = (f32[960,128]{1,0:T(8,128)}, f32[960,128]{1,0:T(8,128)}) custom-call(f32[960,128]{1,0:T(8,128)} %bitcast.4, f32[960,128]{1,0:T(8,128)} %bitcast.5, f32[2,8,128]{2,1,0:T(8,128)} %mean_in.1, f32[7,2,8,128]{3,2,1,0:T(8,128)} %fluct_in.1, s32[3,1680]{1,0:T(4,128)} %triples_in.1, f32[1680]{0:T(1024)} %coupling_in.1), custom_call_target="tpu_custom_call" | custom-call | tf_op jit(solution)/shard_map/pallas_call | solution.py:471
  39.4 2.2 %broadcast_multiply_fusion = (f32[960,128]{1,0:T(8,128)}, f32[960,128]{1,0:T(8,128)}) fusion(f32[960,128]{1,0:T(8,128)} %get-tuple-element.5, f32[960,128]{1,0:T(8,128)} %get-tuple-element.4), kind=kLoop, calls=%fused_computation | loop fusion | flops 245760 | bytes 1966080 | tf_op jit(solution)/shard_map/mul | solution.py:517
